TPU v7x, 256 devices: a whole 4x4x8 slice. The times are simulated.
256 devices in a mesh: ctx: 32 (over z, x), head: 8 (over y, core).
Axes of the slice: x: 4, y: 4, z: 8, core: 2. Of those that a mesh axis runs over, the one named last changes fastest.
Arguments:
- latent_cache: bfloat16 [2048, 36864], P('ctx'), may hold values from -6 to 6
- queries: bfloat16 [4096, 24576], P('ctx', 'head'), may hold values from -320 to 320
- chosen: int32 [4096, 32], P('ctx'), may hold values from 0 to 2047, as said below
- key_up: bfloat16 [128, 128, 512], P('head'), may hold values from -0.5 to 0.5
- value_up: bfloat16 [128, 512, 128], P('head'), may hold values from -2.390625 to 2.390625
Outputs:
- attended: bfloat16 [4096, 16384], P('ctx', 'head')
Inputs may be any that keep to these rules, and one draw needn't show every extreme that they name: `chosen`: A query's 32 blocks are distinct. The queries of one ctx index (aligned blocks of 128 rows) choose exactly 44 distinct blocks together; at most 3 of them lie in one ctx index's 64 cache blocks, and exactly 3 in the newest 64 blocks.
All inputs are finite; a program needn't handle non-finite values.
Results may differ from a plain program's by a relative error of at most 0.0095.
Values may be sent and summed in bfloat16 or wider, within the bound.
A program may use at most 128 MiB of HBM per device.

v0:
```python
import math

import jax
import jax.numpy as jnp
from jax import lax
from jax.sharding import PartitionSpec as P

BLOCK = 64
POOL = 44


def slot_table(block_flags, capacity):
    ranking = jnp.cumsum(block_flags, axis=1) - 1
    columns = jnp.arange(capacity, dtype=jnp.int32)
    matched = (block_flags[:, :, None] == 1) & (ranking[:, :, None] == columns[None, None, :])
    offsets = jnp.arange(block_flags.shape[1], dtype=jnp.int32)[None, :, None]
    located = jnp.sum(jnp.where(matched, offsets, 0), axis=1)
    present = jnp.any(matched, axis=1)
    return jnp.where(present, located, -1)


def on_device(latent_cache, queries, chosen, key_up, value_up):
    ctx_count = lax.axis_size("ctx")
    blocks_dev = latent_cache.shape[0]
    heads_dev = key_up.shape[0]
    nope_dim = key_up.shape[1]
    latent_dim = key_up.shape[2]
    row_width = latent_cache.shape[1] // BLOCK
    rope_dim = row_width - latent_dim
    capacity = max(3, (2 * POOL + ctx_count - 1) // ctx_count)
    query_count = queries.shape[0]
    heads_view = queries.reshape(query_count, heads_dev, nope_dim + rope_dim)
    latent_query = jnp.einsum(
        "qhn,hnl->qhl", heads_view[:, :, :nope_dim], key_up, preferred_element_type=jnp.float32
    ).astype(jnp.bfloat16)
    full_query = jnp.concatenate([latent_query, heads_view[:, :, nope_dim:]], axis=2)
    flat_picks = chosen.reshape(-1)
    need_flags = (
        jnp.zeros((ctx_count * blocks_dev,), jnp.int32)
        .at[flat_picks]
        .max(1)
        .reshape(ctx_count, blocks_dev)
    )
    wanted = slot_table(need_flags, capacity)
    requested = lax.all_to_all(wanted, "ctx", split_axis=0, concat_axis=0, tiled=True)
    outgoing = latent_cache[jnp.maximum(requested, 0)]
    filled = (wanted >= 0).reshape(-1)
    slot_index = jnp.nonzero(filled, size=POOL)[0]
    block_ids = (jnp.arange(ctx_count, dtype=jnp.int32)[:, None] * blocks_dev + wanted).reshape(-1)[
        slot_index
    ]
    selected = jnp.any(chosen[:, :, None] == block_ids[None, None, :], axis=1)
    score_scale = (nope_dim + rope_dim) ** (-0.5)
    per_step = math.gcd(query_count, max(1, 512 // heads_dev))
    steps_count = query_count // per_step
    initial = (
        jnp.full((query_count, heads_dev), -1e30, jnp.float32),
        jnp.zeros((query_count, heads_dev), jnp.float32),
        jnp.zeros((query_count, heads_dev, latent_dim), jnp.float32),
    )
    fetched = lax.all_to_all(outgoing, "ctx", split_axis=0, concat_axis=0, tiled=True)
    pooled = fetched.reshape(ctx_count * capacity, BLOCK, row_width)[slot_index]
    rows_each = pooled.shape[1]
    keys_flat = pooled.reshape(-1, row_width)
    key_values = keys_flat[:, :latent_dim]
    key_mask = jnp.repeat(selected, rows_each, axis=1)

    def one_step(inputs):
        query_block, mask_block, running_max, running_sum, running_out = inputs
        scores = (
            jnp.einsum("qhr,kr->qhk", query_block, keys_flat, preferred_element_type=jnp.float32)
            * score_scale
        )
        scores = jnp.where(mask_block[:, None, :], scores, -1e30)
        newest = jnp.maximum(running_max, jnp.max(scores, axis=2))
        exponent = jnp.exp(scores - newest[:, :, None])
        factor = jnp.exp(running_max - newest)
        running_sum = running_sum * factor + jnp.sum(exponent, axis=2)
        contrib = jnp.einsum(
            "qhk,kl->qhl",
            exponent.astype(jnp.bfloat16),
            key_values,
            preferred_element_type=jnp.float32,
        )
        running_out = running_out * factor[:, :, None] + contrib
        return (newest, running_sum, running_out)

    results = lax.map(
        one_step,
        (
            full_query.reshape(steps_count, per_step, heads_dev, row_width),
            key_mask.reshape(steps_count, per_step, -1),
            initial[0].reshape(steps_count, per_step, heads_dev),
            initial[1].reshape(steps_count, per_step, heads_dev),
            initial[2].reshape(steps_count, per_step, heads_dev, latent_dim),
        ),
    )
    mixed = (
        results[2].reshape(query_count, heads_dev, latent_dim)
        / results[1].reshape(query_count, heads_dev)[:, :, None]
    ).astype(jnp.bfloat16)
    result = jnp.einsum("qhl,hlv->qhv", mixed, value_up, preferred_element_type=jnp.float32)
    return result.astype(jnp.bfloat16).reshape(query_count, -1)


def solution(mesh):
    return jax.shard_map(
        on_device,
        mesh=mesh,
        in_specs=(
            P("ctx", None),
            P("ctx", "head"),
            P("ctx", None),
            P("head", None, None),
            P("head", None, None),
        ),
        out_specs=P("ctx", "head"),
        check_vma=False,
    )
```

profile of v0, /device:TPU:1, one launch (start us, length us, event | category | flops | bytes accessed | tf_op | source)
XLA Modules:
  0.0 369.8 jit_solution(7003317694225724714)
XLA Ops:
  1.1 24.0 %scatter_custom_fusion = s32[2048]{0:T(1024)S(1)} fusion(s32[4096]{0:T(1024)S(1)} %bitcast.62, s32[4096]{0:T(1024)S(1)} %broadcast.237, s32[]{:T(128)} %copy.89), kind=kCustom, calls=%fused_computation.55 | custom fusion | flops 4096 | bytes 8196 | tf_op jit(solution)/shard_map/scatter-max | solution.py:41
  26.5 20.3 %all_to_all.11 = s32[32,1,3]{2,1,0:T(1,128)S(1)} all-to-all(s32[32,1,3]{2,1,0:T(1,128)S(1)} %copy.62), channel_id=1, replica_groups=mesh['ctx'=32,'head'=8] {'ctx'}, dimensions={0} | all-to-all | bytes 768 | tf_op jit(solution)/shard_map/all_to_all | solution.py:45
  46.9 16.9 %gather_fusion.1 = bf16[96,36864]{1,0:T(8,128)(2,1)} fusion(bf16[64,36864]{1,0:T(8,128)(2,1)} %param.7, s32[1024]{0:T(1024)S(1)} %pad_clamp_fusion), kind=kCustom, calls=%fused_computation.1 | custom fusion | bytes 14156160 | tf_op jit(solution)/shard_map/gather | solution.py:46
  63.8 8.7 %reshape.263 = bf16[32,3,36864]{2,1,0:T(4,128)(2,1)} reshape(bf16[96,36864]{1,0:T(8,128)(2,1)} %gather_fusion.1) | data formatting | bytes 14155776 | tf_op jit(solution)/shard_map/gather | solution.py:46
  72.5 5.1 %all-to-all-start.1 = ((bf16[32,3,36864]{2,1,0:T(4,128)(2,1)}), bf16[32,3,36864]{2,1,0:T(4,128)(2,1)}, u32[]{:S(2)}, u32[]{:S(2)}) async-start(bf16[32,3,36864]{2,1,0:T(4,128)(2,1)} %reshape.263), calls=%async_computation.1 | async-start | bytes 18874368 | tf_op jit(solution)/shard_map/all_to_all | solution.py:61
  86.1 1.6 pad_maximum_fusion
  87.8 4.9 %copy.61 = bf16[128,16,576]{2,1,0:T(8,128)(2,1)} copy(bf16[128,16,576]{0,2,1:T(8,128)(2,1)} %pad_maximum_fusion) | data formatting | bytes 4718592 | tf_op jit(solution)/shard_map/concatenate | solution.py:36
  92.7 200.3 %all-to-all-done.1 = bf16[32,3,36864]{2,1,0:T(4,128)(2,1)} async-done(((bf16[32,3,36864]{2,1,0:T(4,128)(2,1)}), bf16[32,3,36864]{2,1,0:T(4,128)(2,1)}, u32[]{:S(2)}, u32[]{:S(2)}) %all-to-all-start.1) | async-done | bytes 7077920 | tf_op jit(solution)/shard_map/all_to_all | solution.py:61
  293.0 16.0 %reshape.248 = bf16[96,64,576]{2,1,0:T(8,128)(2,1)} reshape(bf16[32,3,36864]{2,1,0:T(4,128)(2,1)} %all-to-all-done.1) | data formatting | bytes 14155776 | tf_op jit(solution)/shard_map/reshape | solution.py:62
  309.0 6.2 %gather_fusion.2 = bf16[44,64,576]{2,1,0:T(8,128)(2,1)} fusion(bf16[96,64,576]{2,1,0:T(8,128)(2,1)} %reshape.248, s32[1024]{0:T(1024)S(1)} %pad_clamp_fusion.1), kind=kCustom, calls=%fused_computation.2 | custom fusion | bytes 6488240 | tf_op jit(solution)/shard_map/gather | solution.py:62
  315.3 5.9 %copy.63 = bf16[2816,576]{0,1:T(8,128)(2,1)} copy(bf16[2816,576]{1,0:T(8,128)(2,1)} %bitcast.55) | data formatting | bytes 6488064 | tf_op jit(solution)/shard_map/while | solution.py:88
  321.2 3.6 slice.20
  324.8 38.1 %while.12 = (s32[]{:T(128)}, f32[4,32,16]{2,1,0:T(8,128)S(1)}, f32[4,32,16,512]{3,2,1,0:T(8,128)}, pred[4,32,2816]{2,1,0:T(8,128)(4,1)S(1)}, bf16[4,32,16,576]{3...) while((s32[]{:T(128)}, f32[4,32,16]{2,1,0:T(8,128)S(1)}, ...), condition=%wide.region_12.13_spmd, body=%wide.region_9.12_spmd.sunk | while | flops 3153463808 | bytes 37184632 | solution.py:88
  324.8 5.0 %fusion.58 = (f32[32,16]{1,0:T(8,128)S(1)}, f32[32,16,2816]{2,1,0:T(8,128)S(1)}) fusion(pred[32,2816]{1,0:T(8,128)(4,1)S(1)} %dynamic-slice_bitcast_fusion.2, bf16[2816,576]{0,1:T(8,128)(2,1)} %get-tuple-element.167, bf16[4,32,16,576]{3,2,1,0:T(8,128)(2,1)} %get-tuple-element.166, s32[]{:T(128)} %get-tuple-element.154), kind=kOutput, calls=%fused_computation.7.clone.1 | convolution fusion | flops 1665269248 | bytes 9759232 | tf_op jit(solution)/shard_map/while/body/eval_jaxpr/qhr,kr->qhk/dot_general | solution.py:71
  329.9 2.8 fusion.60
  332.7 1.5 fusion.59
  334.3 5.0 %fusion.58 = (f32[32,16]{1,0:T(8,128)S(1)}, f32[32,16,2816]{2,1,0:T(8,128)S(1)}) fusion(pred[32,2816]{1,0:T(8,128)(4,1)S(1)} %dynamic-slice_bitcast_fusion.2, bf16[2816,576]{0,1:T(8,128)(2,1)} %get-tuple-element.167, bf16[4,32,16,576]{3,2,1,0:T(8,128)(2,1)} %get-tuple-element.166, s32[]{:T(128)} %get-tuple-element.154), kind=kOutput, calls=%fused_computation.7.clone.1 | convolution fusion | flops 1665269248 | bytes 9759232 | tf_op jit(solution)/shard_map/while/body/eval_jaxpr/qhr,kr->qhk/dot_general | solution.py:71
  339.4 2.8 fusion.60
  342.2 1.5 fusion.59
  343.8 5.0 %fusion.58 = (f32[32,16]{1,0:T(8,128)S(1)}, f32[32,16,2816]{2,1,0:T(8,128)S(1)}) fusion(pred[32,2816]{1,0:T(8,128)(4,1)S(1)} %dynamic-slice_bitcast_fusion.2, bf16[2816,576]{0,1:T(8,128)(2,1)} %get-tuple-element.167, bf16[4,32,16,576]{3,2,1,0:T(8,128)(2,1)} %get-tuple-element.166, s32[]{:T(128)} %get-tuple-element.154), kind=kOutput, calls=%fused_computation.7.clone.1 | convolution fusion | flops 1665269248 | bytes 9759232 | tf_op jit(solution)/shard_map/while/body/eval_jaxpr/qhr,kr->qhk/dot_general | solution.py:71
  348.8 2.8 fusion.60
  353.2 5.0 %fusion.58 = (f32[32,16]{1,0:T(8,128)S(1)}, f32[32,16,2816]{2,1,0:T(8,128)S(1)}) fusion(pred[32,2816]{1,0:T(8,128)(4,1)S(1)} %dynamic-slice_bitcast_fusion.2, bf16[2816,576]{0,1:T(8,128)(2,1)} %get-tuple-element.167, bf16[4,32,16,576]{3,2,1,0:T(8,128)(2,1)} %get-tuple-element.166, s32[]{:T(128)} %get-tuple-element.154), kind=kOutput, calls=%fused_computation.7.clone.1 | convolution fusion | flops 1665269248 | bytes 9759232 | tf_op jit(solution)/shard_map/while/body/eval_jaxpr/qhr,kr->qhk/dot_general | solution.py:71
  358.3 2.8 fusion.60
  362.9 5.8 %fusion.35 = bf16[16,128,128]{1,2,0:T(8,128)(2,1)S(1)} fusion(bf16[16,512,128]{2,1,0:T(8,128)(2,1)} %param.11, f32[128,16,512]{2,1,0:T(8,128)} %bitcast.64, f32[128,16]{0,1:T(8,128)S(1)} %copy.64), kind=kOutput, calls=%fused_computation.35 | convolution fusion | flops 270794752 | bytes 6823936 | tf_op jit(solution)/shard_map/qhl,hlv->qhv/dot_general | solution.py:102
  (68 shorter events, 15.4 us)
Async XLA Ops:
  0.0 85.3 %copy-start = (bf16[16,128,512]{2,1,0:T(8,128)(2,1)S(1)}, bf16[16,128,512]{2,1,0:T(8,128)(2,1)}, u32[]{:S(2)}) copy-start(bf16[16,128,512]{2,1,0:T(8,128)(2,1)} %param.10) | copy-start | bytes 6291460
  72.5 8.7 %copy-start.3 = (s32[128,32]{0,1:T(8,128)S(1)}, s32[128,32]{0,1:T(8,128)}, u32[]{:S(2)}) copy-start(s32[128,32]{0,1:T(8,128)} %param.9) | copy-start | bytes 49156
  72.5 220.5 %all-to-all-start.1 = ((bf16[32,3,36864]{2,1,0:T(4,128)(2,1)}), bf16[32,3,36864]{2,1,0:T(4,128)(2,1)}, u32[]{:S(2)}, u32[]{:S(2)}) async-start(bf16[32,3,36864]{2,1,0:T(4,128)(2,1)} %reshape.263), calls=%async_computation.1 | async-start | bytes 18874368 | tf_op jit(solution)/shard_map/all_to_all | solution.py:61
  324.8 5.1 %copy-start.2 = (bf16[2816,512]{1,0:T(8,128)(2,1)S(1)}, bf16[2816,512]{1,0:T(8,128)(2,1)}, u32[]{:S(2)}) copy-start(bf16[2816,512]{1,0:T(8,128)(2,1)} %get-tuple-element.168) | copy-start | bytes 8650756 | tf_op jit(solution)/shard_map/while
  334.3 5.1 %copy-start.2 = (bf16[2816,512]{1,0:T(8,128)(2,1)S(1)}, bf16[2816,512]{1,0:T(8,128)(2,1)}, u32[]{:S(2)}) copy-start(bf16[2816,512]{1,0:T(8,128)(2,1)} %get-tuple-element.168) | copy-start | bytes 8650756 | tf_op jit(solution)/shard_map/while
  343.8 5.1 %copy-start.2 = (bf16[2816,512]{1,0:T(8,128)(2,1)S(1)}, bf16[2816,512]{1,0:T(8,128)(2,1)}, u32[]{:S(2)}) copy-start(bf16[2816,512]{1,0:T(8,128)(2,1)} %get-tuple-element.168) | copy-start | bytes 8650756 | tf_op jit(solution)/shard_map/while
  353.2 5.1 %copy-start.2 = (bf16[2816,512]{1,0:T(8,128)(2,1)S(1)}, bf16[2816,512]{1,0:T(8,128)(2,1)}, u32[]{:S(2)}) copy-start(bf16[2816,512]{1,0:T(8,128)(2,1)} %get-tuple-element.168) | copy-start | bytes 8650756 | tf_op jit(solution)/shard_map/while
  362.9 6.9 %copy-start.1 = (bf16[16,128,512]{2,1,0:T(8,128)(2,1)S(1)}, bf16[16,128,512]{2,1,0:T(8,128)(2,1)}, u32[]{:S(2)}) copy-start(bf16[16,128,512]{2,1,0:T(8,128)(2,1)} %param.10) | copy-start | bytes 6291460
where the time goes:
time: 371 us; the launch traced here: 370 us
  waiting for transfers between devices  200 us (54%)
  local copies, waits for them, and re-layouts  70 us (19%)
  matrix products  37.9 us (10%)
  other arithmetic  35.6 us (10%)
  blocking collectives  20.3 us (5%)
  starting transfers between devices  5.1 us (1%)
    all_to_all x1, waiting for transfers between devices, on_device(): lax.all_to_all(outgoing, 'ctx', split_axis=0, concat_axis=0, tiled=True)  200 us
    gather x2, local copies, waits for them, and re-layouts, on_device(): outgoing = latent_cache[jnp.maximum(requested, 0)]  25.6 us
    another operation x1, other arithmetic, on_device(): need_flags = jnp.zeros((ctx_count * blocks_dev,), jnp.int32).at[flat_pick...  24 us
    all_to_all x1, blocking collectives, on_device(): lax.all_to_all(wanted, 'ctx', split_axis=0, concat_axis=0, tiled=True)  20.3 us
    dot_general x4, matrix products, one_step(): jnp.einsum('qhr,kr->qhk', query_block, keys_flat, preferred_element_type=...  20.1 us
    reshape x1, local copies, waits for them, and re-layouts, on_device(): pooled = fetched.reshape(ctx_count * capacity, BLOCK, row_width)[slot_index]  16 us
    dot_general x4, matrix products, one_step(): jnp.einsum('qhk,kl->qhl', exponent.astype(jnp.bfloat16), key_values, pref...  11.2 us
  transfers between devices with their start and end apart: 1, of which 1 were waited for; matrix products, arithmetic and copies ran while one was open for 4% of the time, Pallas kernels for 0%

commit v1 on v0

v1 whole, which is shorter than its diff:
```python
import functools

import jax
import jax.numpy as jnp
from jax import lax
from jax.experimental import pallas as pl
from jax.experimental.pallas import tpu as pltpu
from jax.sharding import PartitionSpec as P

BF = jnp.bfloat16
F32 = jnp.float32
CTX = 32
HEADS = 16
ROWS = 128
BD = 64
CAP = 3
POOL = 44
SLOTS = 48
SHARE = 4608
PAIR = 1152
CHUNKS = 4
KEYS = 768
GROUPS = ((0, 2), (2, 2), (4, 2), (6, 1))
HP = 2
HIDE = -1e30
SCALE = (192**-0.5) * 1.4426950408889634


def nn(a, b):
    return lax.dot_general(a, b, (((1,), (0,)), ((), ())), preferred_element_type=F32)


def nt(a, b):
    return lax.dot_general(a, b, (((1,), (1,)), ((), ())), preferred_element_type=F32)


def iota(shape, dim):
    return lax.broadcasted_iota(jnp.int32, shape, dim)


def ones(cond):
    return jnp.where(cond, 1.0, 0.0).astype(BF)


def slot_of_row(r):
    return jnp.where(r < 5, 0, jnp.where(r < 10, 1, 2))


def kernel(
    cache_hbm, queries_hbm, chosen_hbm, kup_hbm, vup_hbm, out_ref,
    shard, qraw, picks, kup, vup, req_send, req_recv, pack_send, pack_recv,
    pool, rext, qext, acc, top, total,
    in_sem, req_sem, pack_ssem, pack_rsem, gat_ssem, gat_rsem,
):
    me = lax.axis_index("ctx")
    hd = lax.axis_index("head")
    core = lax.rem(hd, 2)
    up = lax.rem(hd + 2, 8)
    down = lax.rem(hd + 6, 8)
    mate = hd + 1 - 2 * core
    far = lax.rem(hd + 4, 8)

    loads = []
    for n, (src, dst) in enumerate(
        (
            (chosen_hbm, picks),
            (cache_hbm.at[:, pl.ds(pl.multiple_of(hd * SHARE, 128), SHARE)], shard),
            (queries_hbm, qraw),
            (kup_hbm, kup),
            (vup_hbm, vup),
        )
    ):
        load = pltpu.make_async_copy(src, dst, in_sem.at[n])
        load.start()
        loads.append(load)

    barrier = pltpu.get_barrier_semaphore()

    def greet(k, carry):
        pl.semaphore_signal(barrier, inc=1, device_id={"ctx": lax.rem(me + k, CTX)})
        return carry

    lax.fori_loop(1, CTX, greet, 0)
    for peer in (up, down, mate):
        pl.semaphore_signal(barrier, inc=1, device_id={"head": peer})

    loads[0].wait()
    pick = picks[...]
    eye = ones(iota((32, 32), 0) == iota((32, 32), 1))
    hi_t = nt(eye, lax.shift_right_logical(pick, 6).astype(F32).astype(BF))
    lo_t = nt(eye, (pick & 63).astype(F32).astype(BF))
    own_i = iota((CTX, ROWS), 0).astype(F32)
    blk_i = (iota((128, ROWS), 0) & 63).astype(F32)
    hi_oh = jnp.concatenate([ones(hi_t[j : j + 1] == own_i) for j in range(32)], axis=1)
    lo_oh = jnp.concatenate([ones(lo_t[j : j + 1] == blk_i) for j in range(32)], axis=1)
    flags = ones(nt(hi_oh, lo_oh) > 0.5)
    lane_r, lane_c = iota((128, 128), 0), iota((128, 128), 1)
    upto = ones((lane_r <= lane_c) & ((lane_r >> 6) == (lane_c >> 6)))
    rank = nn(flags, upto)
    hit = [(flags.astype(F32) > 0.5) & (rank == float(c + 1)) for c in range(CAP)]
    rep = ones((iota((CTX * 16, CTX), 0) >> 4) == iota((CTX * 16, CTX), 1))
    x0, x1, x2 = [nn(rep, ones(h)) for h in hit]
    row = iota((CTX * 16, 128), 0) & 15
    lane = iota((CTX * 16, 128), 1)
    last = jnp.where(lane < 64, x0, x1)
    first = jnp.where(row < 5, x0, jnp.where(row < 10, x1, jnp.where(row < 15, x2, last)))
    req_send[:, :128] = first.astype(BF)
    req_send[:, 128:] = jnp.where(row == 15, x2, 0.0).astype(BF)
    mine = pl.ds(pl.multiple_of(me * 16, 16), 16)
    req_recv[mine, :] = req_send[mine, :]

    pl.semaphore_wait(barrier, CTX - 1 + 3)

    def ask(k, carry):
        to = lax.rem(me + k, CTX)
        pltpu.make_async_remote_copy(
            src_ref=req_send.at[pl.ds(pl.multiple_of(to * 16, 16), 16), :],
            dst_ref=req_recv.at[mine, :],
            send_sem=req_sem.at[0],
            recv_sem=req_sem.at[1],
            device_id={"ctx": to},
        ).start()
        return carry

    lax.fori_loop(1, CTX, ask, 0)

    n_lane = nt(jnp.ones((8, 128), BF), flags) * 0.5
    wide_o, wide_l = iota((CTX, CTX * 16), 0), iota((CTX, CTX * 16), 1) >> 4
    count = nn(n_lane.astype(BF), ones(wide_o == wide_l))[:1]
    base = nn(n_lane.astype(BF), ones(wide_o < wide_l))[:1]
    row_l = iota((1, CTX * 16), 1) & 15
    slot_s = iota((SLOTS, CTX * 16), 0).astype(F32)

    def place(c, rows):
        return ones(jnp.where(rows & (c < count), base + c, -1.0) == slot_s)

    c_row = slot_of_row(row_l)
    part = row_l - 5 * c_row
    spread = jnp.concatenate(
        [place(c_row.astype(F32), (row_l < 15) & (part == i)) for i in range(5)], axis=0
    )
    rest = [place(float(c), row_l == 15) for c in range(CAP)]

    n_col = nn(flags, jnp.ones((128, 128), BF)) * 0.5
    before = ones(iota((CTX, CTX), 1) < iota((CTX, CTX), 0))
    base_col = nn(before, n_col.astype(BF))
    lane32 = iota((CTX, 128), 1)
    block_ids = jnp.zeros((1, 128), F32)
    for c in range(CAP):
        lo_c = jnp.sum(
            jnp.where(hit[c] & (lane32 < 64), lane32, 0).astype(F32), axis=1, keepdims=True
        )
        at = (base_col + float(c) == lane32.astype(F32)) & (n_col > float(c))
        ident = iota((CTX, 128), 0).astype(F32) * 64.0 + lo_c
        block_ids = block_ids + jnp.sum(jnp.where(at, ident, 0.0), axis=0, keepdims=True)
    ids = jnp.broadcast_to(block_ids, (ROWS, 128))
    pick_f = pick.astype(F32)
    found = jnp.zeros((ROWS, 128), F32)
    for j in range(32):
        found = jnp.where(pick_f[:, j : j + 1] == ids, 1.0, found)
    slot_l = iota((ROWS, 128), 1)
    hide = jnp.where((slot_l < SLOTS) & ((found < 0.5) | (slot_l >= POOL)), HIDE, 0.0).astype(BF)

    loads[1].wait()
    pltpu.make_async_remote_copy(
        src_ref=req_send.at[pl.ds(0, (CTX - 1) * 16), :],
        dst_ref=req_recv.at[pl.ds(0, (CTX - 1) * 16), :],
        send_sem=req_sem.at[0],
        recv_sem=req_sem.at[1],
        device_id={"ctx": me},
    ).wait_recv()
    got0, got1 = req_recv[:, :128], req_recv[:, 128:]
    part_r = row - 5 * slot_of_row(row)
    sel = [
        jnp.where((part_r == 2 * k + (lane >> 6)) & (row < 15), got0.astype(F32), 0.0).astype(BF)
        for k in range(3)
    ]
    tail_row = row == 15
    tail = [
        jnp.where(tail_row & (lane < 64), got0.astype(F32), 0.0).astype(BF),
        jnp.where(tail_row & (lane >= 64), got0.astype(F32), 0.0).astype(BF),
        jnp.where(tail_row & (lane < 64), got1.astype(F32), 0.0).astype(BF),
    ]
    base_sel = jnp.concatenate(sel, axis=1)

    def tile(u):
        return shard[:, u * 128 : u * 128 + 128]

    for g, (t0, n) in enumerate(GROUPS):
        for t in range(t0, t0 + n):
            src = [tile(5 * t + i) for i in range(5)] + [tile(35)]
            if t < 4:
                packed = nn(base_sel, jnp.concatenate(src, axis=0))
            else:
                packed = nn(
                    jnp.concatenate([base_sel, tail[t - 4]], axis=1),
                    jnp.concatenate(src + [tile(35)] * 2, axis=0),
                )
            pack_send[t] = packed.astype(BF)
        pack_recv[t0 : t0 + n, mine, :] = pack_send[t0 : t0 + n, mine, :]

        def give(k, carry, g=g, t0=t0, n=n):
            to = lax.rem(me + k, CTX)
            pltpu.make_async_remote_copy(
                src_ref=pack_send.at[pl.ds(t0, n), pl.ds(pl.multiple_of(to * 16, 16), 16), :],
                dst_ref=pack_recv.at[pl.ds(t0, n), mine, :],
                send_sem=pack_ssem.at[g],
                recv_sem=pack_rsem.at[g],
                device_id={"ctx": to},
            ).start()
            return carry

        lax.fori_loop(1, CTX, give, 0)

    loads[2].wait()
    loads[3].wait()
    lane_q = iota((ROWS, 128), 1)
    for pair in range(HEADS // 2):
        a, b, c = [
            qraw[:, (3 * pair + i) * 128 : (3 * pair + i + 1) * 128].astype(F32) for i in range(3)
        ]
        b_r, c_r = pltpu.roll(b, 64, 1), pltpu.roll(c, 64, 1)
        halves = (
            (a, jnp.where(lane_q < 64, b, b_r)),
            (jnp.where(lane_q < 64, b_r, c_r), jnp.where(lane_q < 64, c_r, c)),
        )
        for k, (nope, rope) in enumerate(halves):
            h = 2 * pair + k
            qext[h, :, :512] = nn(nope.astype(BF), kup[h]).astype(BF)
            qext[h, :, 512:640] = rope.astype(BF)
            qext[h, :, 640:] = hide
    slot_k = iota((8, SLOTS, 128), 1)
    lane_k = iota((8, SLOTS, 128), 2)
    for j in range(2):
        rext[j, :, 128:] = jnp.concatenate([ones(slot_k == lane_k).reshape(384, 128)] * 2, axis=0)

    def gather_copy(j, kind, piece, to):
        return pltpu.make_async_remote_copy(
            src_ref=pool.at[j, piece],
            dst_ref=pool.at[j, piece],
            send_sem=gat_ssem.at[j, kind],
            recv_sem=gat_rsem.at[j, kind],
            device_id={"head": to},
        )

    started = []

    def send(j, kind, piece, to):
        copy = gather_copy(j, kind, piece, to)
        copy.start()
        started.append(copy)

    tiles = {}
    lane48 = iota((SLOTS, 128), 1)

    def arrive(j):
        t0, n = GROUPS[j]
        pltpu.make_async_remote_copy(
            src_ref=pack_send.at[pl.ds(t0, n), pl.ds(0, (CTX - 1) * 16), :],
            dst_ref=pack_recv.at[pl.ds(t0, n), pl.ds(0, (CTX - 1) * 16), :],
            send_sem=pack_ssem.at[j],
            recv_sem=pack_rsem.at[j],
            device_id={"ctx": me},
        ).wait_recv()
        for t in range(t0, t0 + n):
            moved = nn(spread, pack_recv[t])
            for i in range(5):
                tiles[5 * t + i] = moved[SLOTS * i : SLOTS * i + SLOTS]
        if j == CHUNKS - 1:
            tiles[35] = sum(nn(rest[c], pack_recv[4 + c]) for c in range(CAP))
        w = [tiles[9 * j + i] for i in range(9)]
        r = [pltpu.roll(x, 64, 1) for x in w[4:]]
        cols = w[:4] + [jnp.where(lane48 < 64, r[k], r[k + 1]) for k in range(4)]
        cols.append(jnp.where(lane48 < 64, w[4], w[8]))
        pool[j, hd] = jnp.concatenate(cols, axis=1).astype(BF)
        send(j, 0, hd, up)
        send(j, 1, hd, down)
        send(j, 3, hd, mate)

    def relay_near(j):
        gather_copy(j, 0, down, up).wait_recv()
        gather_copy(j, 1, up, down).wait_recv()
        send(j, 2, lax.rem(hd + 6 + 4 * core, 8), lax.rem(hd + 2 + 4 * core, 8))
        send(j, 4, down, mate)
        send(j, 5, up, mate)

    def relay_far(j):
        gather_copy(j, 2, far, up).wait_recv()
        send(j, 6, far, mate)

    def ready(j):
        for kind in (3, 4, 5, 6):
            gather_copy(j, kind, mate, mate).wait_recv()
        rope = pool[j, :, :, 1024:].reshape(384, 128).astype(F32)
        lane_p = iota((384, 128), 1)
        rext[j % 2, :384, :128] = jnp.where(lane_p < 64, rope, 0.0).astype(BF)
        rext[j % 2, 384:, :128] = jnp.where(lane_p < 64, 0.0, rope).astype(BF)

    rows_step = HP * ROWS

    def attend(j, lo, hi):
        def step(n, carry):
            hs = pl.ds(n * HP, HP)
            keys = jnp.concatenate(
                [pool[j, :, :, :512].reshape(384, 512), pool[j, :, :, 512:1024].reshape(384, 512)],
                axis=0,
            )
            q = qext[hs].reshape(rows_step, 768)
            s = nt(q, jnp.concatenate([keys, rext[j % 2]], axis=1))
            m_new = jnp.broadcast_to(jnp.max(s, axis=1, keepdims=True), (rows_step, 128))
            if j > 0:
                m_old = top[hs].reshape(rows_step, 128)
                m_new = jnp.maximum(m_new, m_old)
            e = jnp.exp2((s - jnp.concatenate([m_new] * 6, axis=1)) * SCALE)
            part_sum = sum(e[:, 128 * k : 128 * k + 128] for k in range(6))
            o = nn(e.astype(BF), keys)
            if j > 0:
                alpha = jnp.exp2((m_old - m_new) * SCALE)
                part_sum = part_sum + total[hs].reshape(rows_step, 128) * alpha
                o = o + acc[hs].reshape(rows_step, 512) * jnp.concatenate([alpha] * 4, axis=1)
            if j < CHUNKS - 1:
                top[hs] = m_new.reshape(HP, ROWS, 128)
                total[hs] = part_sum.reshape(HP, ROWS, 128)
                acc[hs] = o.reshape(HP, ROWS, 512)
            else:
                mixed = (o / jnp.sum(part_sum, axis=1, keepdims=True)).astype(BF)
                for k in range(HP):
                    h = n * HP + k
                    out_ref[:, pl.ds(pl.multiple_of(h * 128, 128), 128)] = nn(
                        mixed[k * ROWS : (k + 1) * ROWS], vup[h]
                    ).astype(BF)
            return carry

        lax.fori_loop(lo, hi, step, 0)

    steps = HEADS // HP
    arrive(0)
    relay_near(0)
    relay_far(0)
    for j in range(CHUNKS):
        ready(j)
        if j == CHUNKS - 1:
            loads[4].wait()
            attend(j, 0, steps)
        else:
            attend(j, 0, steps // 4)
            arrive(j + 1)
            attend(j, steps // 4, steps // 2)
            relay_near(j + 1)
            attend(j, steps // 2, steps)
            relay_far(j + 1)

    for copy in started:
        copy.wait_send()
    pltpu.make_async_remote_copy(
        src_ref=req_send.at[pl.ds(0, (CTX - 1) * 16), :],
        dst_ref=req_recv.at[pl.ds(0, (CTX - 1) * 16), :],
        send_sem=req_sem.at[0],
        recv_sem=req_sem.at[1],
        device_id={"ctx": me},
    ).wait_send()
    for j, (t0, n) in enumerate(GROUPS):
        pltpu.make_async_remote_copy(
            src_ref=pack_send.at[pl.ds(t0, n), pl.ds(0, (CTX - 1) * 16), :],
            dst_ref=pack_recv.at[pl.ds(t0, n), pl.ds(0, (CTX - 1) * 16), :],
            send_sem=pack_ssem.at[j],
            recv_sem=pack_rsem.at[j],
            device_id={"ctx": me},
        ).wait_send()


def on_device(latent_cache, queries, chosen, key_up, value_up):
    any_spec = pl.BlockSpec(memory_space=pl.ANY)
    return pl.pallas_call(
        kernel,
        out_shape=jax.ShapeDtypeStruct((ROWS, HEADS * 128), BF),
        in_specs=[any_spec] * 5,
        out_specs=pl.BlockSpec(memory_space=pltpu.VMEM),
        scratch_shapes=[
            pltpu.VMEM((BD, SHARE), BF),
            pltpu.VMEM((ROWS, HEADS * 192), BF),
            pltpu.VMEM((ROWS, 32), jnp.int32),
            pltpu.VMEM((HEADS, 128, 512), BF),
            pltpu.VMEM((HEADS, 512, 128), BF),
            pltpu.VMEM((CTX * 16, 256), BF),
            pltpu.VMEM((CTX * 16, 256), BF),
            pltpu.VMEM((7, CTX * 16, 128), BF),
            pltpu.VMEM((7, CTX * 16, 128), BF),
            pltpu.VMEM((CHUNKS, 8, SLOTS, PAIR), BF),
            pltpu.VMEM((2, KEYS, 256), BF),
            pltpu.VMEM((HEADS, ROWS, 768), BF),
            pltpu.VMEM((HEADS, ROWS, 512), F32),
            pltpu.VMEM((HEADS, ROWS, 128), F32),
            pltpu.VMEM((HEADS, ROWS, 128), F32),
            pltpu.SemaphoreType.DMA((5,)),
            pltpu.SemaphoreType.DMA((2,)),
            pltpu.SemaphoreType.DMA((CHUNKS,)),
            pltpu.SemaphoreType.DMA((CHUNKS,)),
            pltpu.SemaphoreType.DMA((CHUNKS, 7)),
            pltpu.SemaphoreType.DMA((CHUNKS, 7)),
        ],
        compiler_params=pltpu.CompilerParams(
            collective_id=0, has_side_effects=True, vmem_limit_bytes=56 * 1024 * 1024
        ),
        cost_estimate=pl.CostEstimate(
            flops=15_000_000_000, bytes_accessed=8_000_000, transcendentals=6_300_000
        ),
        name="sparse_latent_attention",
    )(latent_cache, queries, chosen, key_up, value_up)


def solution(mesh):
    return jax.shard_map(
        on_device,
        mesh=mesh,
        in_specs=(
            P("ctx", None),
            P("ctx", "head"),
            P("ctx", None),
            P("head", None, None),
            P("head", None, None),
        ),
        out_specs=P("ctx", "head"),
        check_vma=False,
    )
```

time: 371 us -> 93.4 us (0.25)
  waiting for transfers between devices: 200 us -> 0 us
  Pallas kernels: 0 us -> 89.9 us
  local copies, waits for them, and re-layouts: 70 us -> 3.33 us
  matrix products: 37.9 us -> 0 us
  other arithmetic: 35.6 us -> 0 us
  blocking collectives: 20.3 us -> 0 us
  starting transfers between devices: 5.1 us -> 0 us
    all_to_all x1 -> x0, waiting for transfers between devices: 200 us -> none  [on_device(): lax.all_to_all(outgoing, 'ctx', split_axis=0, concat_axis=0, tiled=True)]
    pallas_call x0 -> x1, Pallas kernels: none -> 89.9 us  [on_device(): pl.pallas_call(kernel, out_shape=jax.ShapeDtypeStruct((ROWS, HEADS * 128)...]
    dot_general x10 -> x0, matrix products: 37.9 us -> none  [the longest x4 20.1 us: one_step(): jnp.einsum('qhr,kr->qhk', query_block, keys_flat, preferred_element_type=...]
    gather x4 -> x0, local copies, waits for them, and re-layouts: 32.6 us -> none  [the longest x2 25.6 us: on_device(): outgoing = latent_cache[jnp.maximum(requested, 0)]]
    another operation x5 -> x0, other arithmetic: 24.3 us -> none  [the longest x1 24 us: on_device(): need_flags = jnp.zeros((ctx_count * blocks_dev,), jnp.int32).at[flat_pick...]
    all_to_all x1 -> x0, blocking collectives: 20.3 us -> none  [on_device(): lax.all_to_all(wanted, 'ctx', split_axis=0, concat_axis=0, tiled=True)]
    reshape x3 -> x0, local copies, waits for them, and re-layouts: 17.1 us -> none  [the longest x1 16 us: on_device(): pooled = fetched.reshape(ctx_count * capacity, BLOCK, row_width)[slot_index]]
    reduce_sum x6 -> x0, other arithmetic: 6.92 us -> none  [the longest x4 6.11 us: one_step(): running_sum = running_sum * factor + jnp.sum(exponent, axis=2)]
  transfers between devices with their start and end apart: 1 -> 0, of which waited for: 1 -> 0; matrix products, arithmetic and copies ran while one was open for 4% -> 0% of each run, Pallas kernels for 0% -> 0%
where the time goes in v1:
time: 93.4 us; the launch traced here: 93.2 us
  Pallas kernels  89.9 us (96%)
  local copies, waits for them, and re-layouts  3.33 us (4%)
    pallas_call x1, Pallas kernels, on_device(): pl.pallas_call(kernel, out_shape=jax.ShapeDtypeStruct((ROWS, HEADS * 128)...  89.9 us
    unnamed x2, local copies, waits for them, and re-layouts  3.33 us

profile of v1, /device:TPU:1, one launch (start us, length us, event | category | flops | bytes accessed | tf_op | source)
XLA Modules:
  0.0 93.2 jit_solution(4018265425764548699)
XLA Ops:
  0.0 1.4 %copy.6.chosen_hbm = s32[128,32]{1,0:T(8,128)} copy(s32[128,32]{0,1:T(8,128)} %param.7) | data formatting | bytes 32768 | tf_op args[2]
  1.4 89.9 %sparse_latent_attention.1 = bf16[128,2048]{1,0:T(8,128)(2,1)} custom-call(bf16[64,36864]{1,0:T(8,128)(2,1)} %cache_hbm.1, bf16[128,3072]{1,0:T(8,128)(2,1)} %queries_hbm.1, s32[128,32]{1,0:T(8,128)} %copy.6.chosen_hbm, bf16[16,128,512]{2,1,0:T(8,128)(2,1)} %kup_hbm.1, bf16[16,512,128]{2,1,0:T(8,128)(2,1)} %vup_hbm.1), custom_call_target="tpu_custom_call" | custom-call | flops 15000000512 | bytes 8000000 | tf_op jit(solution)/shard_map/sparse_latent_attention/pallas_call | solution.py:374
  91.3 1.9 %copy.8 = bf16[128,2048]{1,0:T(8,128)(2,1)} copy(bf16[128,2048]{1,0:T(8,128)(2,1)} %sparse_latent_attention.1) | data formatting | bytes 1048576

commit v2 on v1

v2 whole, which is shorter than its diff:
```python
import functools

import jax
import jax.numpy as jnp
from jax import lax
from jax.experimental import pallas as pl
from jax.experimental.pallas import tpu as pltpu
from jax.sharding import PartitionSpec as P

BF = jnp.bfloat16
F32 = jnp.float32
CTX = 32
HEADS = 16
ROWS = 128
BD = 64
CAP = 3
POOL = 44
SLOTS = 48
SHARE = 4608
PAIR = 1152
CHUNKS = 4
KEYS = 768
GROUPS = ((0, 1), (1, 1), (2, 2), (4, 2), (6, 1))
AHEAD = 3
HP = 8
HIDE = -1e30
SCALE = (192**-0.5) * 1.4426950408889634


def nn(a, b):
    return lax.dot_general(a, b, (((1,), (0,)), ((), ())), preferred_element_type=F32)


def nt(a, b):
    return lax.dot_general(a, b, (((1,), (1,)), ((), ())), preferred_element_type=F32)


def iota(shape, dim):
    return lax.broadcasted_iota(jnp.int32, shape, dim)


def ones(cond):
    return jnp.where(cond, 1.0, 0.0).astype(BF)


def slot_of_row(r):
    return jnp.where(r < 5, 0, jnp.where(r < 10, 1, 2))


def kernel(
    cache_hbm, queries_hbm, chosen_hbm, kup_hbm, vup_hbm, out_ref,
    shard, qraw, picks, kup, vup, req_send, req_recv, pack_send, pack_recv,
    pool, first, rext, qext, acc, top, total,
    in_sem, req_sem, pack_ssem, pack_rsem, gat_ssem, gat_rsem,
):
    me = lax.axis_index("ctx")
    hd = lax.axis_index("head")
    core = lax.rem(hd, 2)
    up = lax.rem(hd + 2, 8)
    down = lax.rem(hd + 6, 8)
    mate = hd + 1 - 2 * core
    far = lax.rem(hd + 4, 8)

    loads = []
    for n, (src, dst) in enumerate(
        (
            (chosen_hbm, picks),
            (cache_hbm.at[:, pl.ds(pl.multiple_of(hd * SHARE, 128), SHARE)], shard),
            (queries_hbm, qraw),
            (kup_hbm, kup),
            (vup_hbm, vup),
        )
    ):
        load = pltpu.make_async_copy(src, dst, in_sem.at[n])
        load.start()
        loads.append(load)

    barrier = pltpu.get_barrier_semaphore()

    def greet(k, carry):
        pl.semaphore_signal(barrier, inc=1, device_id={"ctx": lax.rem(me + k, CTX)})
        return carry

    lax.fori_loop(1, CTX, greet, 0)
    for peer in (up, down, far, mate):
        pl.semaphore_signal(barrier, inc=1, device_id={"head": peer})

    loads[0].wait()
    pick = picks[...]
    hi, lo = lax.shift_right_logical(pick, 6), pick & 63
    own_i = iota((CTX, ROWS), 0)
    blk_i = iota((128, ROWS), 0) & 63
    hi_oh = jnp.concatenate([ones(hi[j : j + 1] == own_i) for j in range(32)], axis=1)
    lo_oh = jnp.concatenate([ones(lo[j : j + 1] == blk_i) for j in range(32)], axis=1)
    flags = ones(nt(hi_oh, lo_oh) > 0.5)
    lane_r, lane_c = iota((128, 128), 0), iota((128, 128), 1)
    upto = ones((lane_r <= lane_c) & ((lane_r >> 6) == (lane_c >> 6)))
    rank = nn(flags, upto)
    hit = [(flags.astype(F32) > 0.5) & (rank == float(c + 1)) for c in range(CAP)]
    rep = ones((iota((CTX * 16, CTX), 0) >> 4) == iota((CTX * 16, CTX), 1))
    x0, x1, x2 = [nn(rep, ones(h)) for h in hit]
    row = iota((CTX * 16, 128), 0) & 15
    lane = iota((CTX * 16, 128), 1)
    req_send[...] = jnp.where(row < 5, x0, jnp.where(row < 10, x1, x2)).astype(BF)
    mine = pl.ds(pl.multiple_of(me * 16, 16), 16)
    req_recv[mine, :] = req_send[mine, :]

    pl.semaphore_wait(barrier, CTX - 1 + 4)

    def ask(k, carry):
        to = lax.rem(me + k, CTX)
        pltpu.make_async_remote_copy(
            src_ref=req_send.at[pl.ds(pl.multiple_of(to * 16, 16), 16), :],
            dst_ref=req_recv.at[mine, :],
            send_sem=req_sem.at[0],
            recv_sem=req_sem.at[1],
            device_id={"ctx": to},
        ).start()
        return carry

    lax.fori_loop(1, CTX, ask, 0)

    n_lane = nt(jnp.ones((8, 128), BF), flags) * 0.5
    wide_o, wide_l = iota((CTX, CTX * 16), 0), iota((CTX, CTX * 16), 1) >> 4
    count = nn(n_lane.astype(BF), ones(wide_o == wide_l))[:1]
    base = nn(n_lane.astype(BF), ones(wide_o < wide_l))[:1]
    row_l = iota((1, CTX * 16), 1) & 15
    slot_s = iota((SLOTS, CTX * 16), 0).astype(F32)

    def place(c, rows):
        return ones(jnp.where(rows & (c < count), base + c, -1.0) == slot_s)

    c_row = slot_of_row(row_l)
    part = row_l - 5 * c_row
    spread = jnp.concatenate(
        [place(c_row.astype(F32), (row_l < 15) & (part == i)) for i in range(5)], axis=0
    )
    rest = [place(float(c), row_l == 15) for c in range(CAP)]

    n_row = n_lane[:1]
    base_row = nn(n_lane.astype(BF), ones(iota((CTX, CTX), 0) < iota((CTX, CTX), 1)))[:1]
    lane_v = iota((8, 128), 1)
    block_v = jnp.where(lane_v < 64, lane_v, 0).astype(F32).astype(BF)
    slot_c = iota((SLOTS, CTX), 0).astype(F32)
    owner_v = iota((1, CTX), 1).astype(F32) * 64.0
    ids = jnp.zeros((SLOTS, CTX), F32)
    for c in range(CAP):
        ident = owner_v + nt(block_v, ones(hit[c]))[:1]
        at = jnp.where(float(c) < n_row, base_row + float(c), -1.0) == slot_c
        ids = ids + jnp.where(at, ident, 0.0)
    ids = jnp.broadcast_to(jnp.sum(ids, axis=1, keepdims=True), (SLOTS, ROWS))
    pick_f = pick.astype(F32)
    found = jnp.zeros((SLOTS, ROWS), F32)
    for j in range(32):
        found = jnp.where(pick_f[j : j + 1] == ids, 1.0, found)
    hidden = jnp.where((found < 0.5) | (iota((SLOTS, ROWS), 0) >= POOL), HIDE, 0.0)
    hide = jnp.concatenate([hidden, jnp.zeros((ROWS - SLOTS, ROWS), F32)], axis=0).T.astype(BF)

    loads[2].wait()
    loads[3].wait()
    lane_q = iota((ROWS, 128), 1)
    for pair in range(HEADS // 2):
        a, b, c = [
            qraw[:, (3 * pair + i) * 128 : (3 * pair + i + 1) * 128].astype(F32) for i in range(3)
        ]
        b_r, c_r = pltpu.roll(b, 64, 1), pltpu.roll(c, 64, 1)
        halves = (
            (a, jnp.where(lane_q < 64, b, b_r)),
            (jnp.where(lane_q < 64, b_r, c_r), jnp.where(lane_q < 64, c_r, c)),
        )
        for k, (nope, rope) in enumerate(halves):
            h = 2 * pair + k
            qext[h, :, :512] = nn(nope.astype(BF), kup[h]).astype(BF)
            qext[h, :, 512:640] = rope.astype(BF)
            qext[h, :, 640:] = hide
    slot_k = iota((8, SLOTS, 128), 1)
    lane_k = iota((8, SLOTS, 128), 2)
    for j in range(2):
        rext[j, :, 128:] = jnp.concatenate([ones(slot_k == lane_k).reshape(384, 128)] * 2, axis=0)

    loads[1].wait()
    pltpu.make_async_remote_copy(
        src_ref=req_send.at[pl.ds(0, (CTX - 1) * 16), :],
        dst_ref=req_recv.at[pl.ds(0, (CTX - 1) * 16), :],
        send_sem=req_sem.at[0],
        recv_sem=req_sem.at[1],
        device_id={"ctx": me},
    ).wait_recv()
    got = req_recv[...].astype(F32)
    part_r = row - 5 * slot_of_row(row)
    sel = [
        jnp.where((part_r == 2 * k + (lane >> 6)) & (row < 15), got, 0.0).astype(BF)
        for k in range(3)
    ]
    tail = [
        jnp.where((row == 15) & (lane < 64), pltpu.roll(got, 15 - 5 * c, 0), 0.0).astype(BF)
        for c in range(CAP)
    ]
    base_sel = jnp.concatenate(sel, axis=1)

    def tile(u):
        return shard[:, u * 128 : u * 128 + 128]

    def give(g):
        t0, n = GROUPS[g]

        def one(k, carry):
            to = lax.rem(me + k, CTX)
            pltpu.make_async_remote_copy(
                src_ref=pack_send.at[pl.ds(t0, n), pl.ds(pl.multiple_of(to * 16, 16), 16), :],
                dst_ref=pack_recv.at[pl.ds(t0, n), mine, :],
                send_sem=pack_ssem.at[g],
                recv_sem=pack_rsem.at[g],
                device_id={"ctx": to},
            ).start()
            return carry

        lax.fori_loop(1, CTX, one, 0)

    for g, (t0, n) in enumerate(GROUPS):
        for t in range(t0, t0 + n):
            src = [tile(5 * t + i) for i in range(5)] + [tile(35)]
            if t < 4:
                packed = nn(base_sel, jnp.concatenate(src, axis=0))
            else:
                packed = nn(
                    jnp.concatenate([base_sel, tail[t - 4]], axis=1),
                    jnp.concatenate(src + [tile(35)] * 2, axis=0),
                )
            pack_send[t] = packed.astype(BF)
        pack_recv[t0 : t0 + n, mine, :] = pack_send[t0 : t0 + n, mine, :]
        if g < AHEAD:
            give(g)


    def gather_copy(g, kind, piece, to):
        part = first.at[g, piece] if g < 2 else pool.at[g - 2, piece]
        return pltpu.make_async_remote_copy(
            src_ref=part,
            dst_ref=part,
            send_sem=gat_ssem.at[g, kind],
            recv_sem=gat_rsem.at[g, kind],
            device_id={"head": to},
        )

    started = []

    def send(g, kind, piece, to):
        copy = gather_copy(g, kind, piece, to)
        copy.start()
        started.append(copy)

    tiles = {}
    lane48 = iota((SLOTS, 128), 1)

    def arrive(g):
        t0, n = GROUPS[g]
        pltpu.make_async_remote_copy(
            src_ref=pack_send.at[pl.ds(t0, n), pl.ds(0, (CTX - 1) * 16), :],
            dst_ref=pack_recv.at[pl.ds(t0, n), pl.ds(0, (CTX - 1) * 16), :],
            send_sem=pack_ssem.at[g],
            recv_sem=pack_rsem.at[g],
            device_id={"ctx": me},
        ).wait_recv()
        for t in range(t0, t0 + n):
            moved = nn(spread, pack_recv[t])
            for i in range(5):
                tiles[5 * t + i] = moved[SLOTS * i : SLOTS * i + SLOTS]
        if g == len(GROUPS) - 1:
            tiles[35] = sum(nn(rest[c], pack_recv[4 + c]) for c in range(CAP))
        u = 9 * max(g - 1, 0)
        even = [tiles[u + k] for k in range(4)]
        if g > 0:
            r = [pltpu.roll(tiles[u + k], 64, 1) for k in range(4, 9)]
            odd = [jnp.where(lane48 < 64, r[k], r[k + 1]) for k in range(4)]
        if g == 0:
            cols = even + [jnp.where(lane48 < 64, tiles[4], 0.0)]
            first[0, hd] = jnp.concatenate(cols, axis=1).astype(BF)
        elif g == 1:
            cols = odd + [jnp.where(lane48 < 64, 0.0, tiles[8])]
            first[1, hd] = jnp.concatenate(cols, axis=1).astype(BF)
        else:
            cols = even + odd + [jnp.where(lane48 < 64, tiles[u + 4], tiles[u + 8])]
            pool[g - 2, hd] = jnp.concatenate(cols, axis=1).astype(BF)
        send(g, 0, hd, up)
        send(g, 1, hd, down)
        send(g, 2, hd, far)
        send(g, 3, hd, mate)
        if g + AHEAD < len(GROUPS):
            give(g + AHEAD)

    def relay(g):
        for kind, piece in ((0, down), (1, up), (2, far)):
            gather_copy(g, kind, piece, piece).wait_recv()
            send(g, 4 + kind, piece, mate)

    def ready(j):
        for g in (0, 1) if j == 0 else (j + 1,):
            for kind in (3, 4, 5, 6):
                gather_copy(g, kind, mate, mate).wait_recv()
        if j == 0:
            rext[0, :384, :128] = first[0, :, :, 512:].reshape(384, 128)
            rext[0, 384:, :128] = first[1, :, :, 512:].reshape(384, 128)
        else:
            rope = pool[j - 1, :, :, 1024:].reshape(384, 128).astype(F32)
            lane_p = iota((384, 128), 1)
            rext[j % 2, :384, :128] = jnp.where(lane_p < 64, rope, 0.0).astype(BF)
            rext[j % 2, 384:, :128] = jnp.where(lane_p < 64, 0.0, rope).astype(BF)

    rows_step = HP * ROWS

    def attend(j, n):
        hs = pl.ds(n * HP, HP)
        if j == 0:
            halves = [first[0, :, :, :512], first[1, :, :, :512]]
        else:
            halves = [pool[j - 1, :, :, :512], pool[j - 1, :, :, 512:1024]]
        keys = jnp.concatenate([x.reshape(384, 512) for x in halves], axis=0)
        q = qext[hs].reshape(rows_step, 768)
        s = nt(q, jnp.concatenate([keys, rext[j % 2]], axis=1))
        m_new = jnp.broadcast_to(jnp.max(s, axis=1, keepdims=True), (rows_step, 128))
        if j > 0:
            m_old = top[hs].reshape(rows_step, 128)
            m_new = jnp.maximum(m_new, m_old)
        e = jnp.exp2((s - jnp.concatenate([m_new] * 6, axis=1)) * SCALE)
        part_sum = sum(e[:, 128 * k : 128 * k + 128] for k in range(6))
        o = nn(e.astype(BF), keys)
        if j > 0:
            alpha = jnp.exp2((m_old - m_new) * SCALE)
            part_sum = part_sum + total[hs].reshape(rows_step, 128) * alpha
            o = o + acc[hs].reshape(rows_step, 512) * jnp.concatenate([alpha] * 4, axis=1)
        if j < CHUNKS - 1:
            top[hs] = m_new.reshape(HP, ROWS, 128)
            total[hs] = part_sum.reshape(HP, ROWS, 128)
            acc[hs] = o.reshape(HP, ROWS, 512)
        else:
            mixed = (o / jnp.sum(part_sum, axis=1, keepdims=True)).astype(BF)
            for k in range(HP):
                h = n * HP + k
                out_ref[:, pl.ds(pl.multiple_of(h * 128, 128), 128)] = nn(
                    mixed[k * ROWS : (k + 1) * ROWS], vup[h]
                ).astype(BF)

    arrive(0)
    arrive(1)
    relay(0)
    arrive(2)
    relay(1)
    ready(0)
    attend(0, 0)
    arrive(3)
    attend(0, 1)
    relay(2)
    arrive(4)
    ready(1)
    attend(1, 0)
    relay(3)
    attend(1, 1)
    ready(2)
    attend(2, 0)
    relay(4)
    attend(2, 1)
    ready(3)
    loads[4].wait()
    attend(3, 0)
    attend(3, 1)

    for copy in started:
        copy.wait_send()
    pltpu.make_async_remote_copy(
        src_ref=req_send.at[pl.ds(0, (CTX - 1) * 16), :],
        dst_ref=req_recv.at[pl.ds(0, (CTX - 1) * 16), :],
        send_sem=req_sem.at[0],
        recv_sem=req_sem.at[1],
        device_id={"ctx": me},
    ).wait_send()
    for j, (t0, n) in enumerate(GROUPS):
        pltpu.make_async_remote_copy(
            src_ref=pack_send.at[pl.ds(t0, n), pl.ds(0, (CTX - 1) * 16), :],
            dst_ref=pack_recv.at[pl.ds(t0, n), pl.ds(0, (CTX - 1) * 16), :],
            send_sem=pack_ssem.at[j],
            recv_sem=pack_rsem.at[j],
            device_id={"ctx": me},
        ).wait_send()


def on_device(latent_cache, queries, chosen, key_up, value_up):
    any_spec = pl.BlockSpec(memory_space=pl.ANY)
    return pl.pallas_call(
        kernel,
        out_shape=jax.ShapeDtypeStruct((ROWS, HEADS * 128), BF),
        in_specs=[any_spec] * 5,
        out_specs=pl.BlockSpec(memory_space=pltpu.VMEM),
        scratch_shapes=[
            pltpu.VMEM((BD, SHARE), BF),
            pltpu.VMEM((ROWS, HEADS * 192), BF),
            pltpu.VMEM((32, ROWS), jnp.int32),
            pltpu.VMEM((HEADS, 128, 512), BF),
            pltpu.VMEM((HEADS, 512, 128), BF),
            pltpu.VMEM((CTX * 16, 128), BF),
            pltpu.VMEM((CTX * 16, 128), BF),
            pltpu.VMEM((7, CTX * 16, 128), BF),
            pltpu.VMEM((7, CTX * 16, 128), BF),
            pltpu.VMEM((CHUNKS - 1, 8, SLOTS, PAIR), BF),
            pltpu.VMEM((2, 8, SLOTS, 640), BF),
            pltpu.VMEM((2, KEYS, 256), BF),
            pltpu.VMEM((HEADS, ROWS, 768), BF),
            pltpu.VMEM((HEADS, ROWS, 512), F32),
            pltpu.VMEM((HEADS, ROWS, 128), F32),
            pltpu.VMEM((HEADS, ROWS, 128), F32),
            pltpu.SemaphoreType.DMA((5,)),
            pltpu.SemaphoreType.DMA((2,)),
            pltpu.SemaphoreType.DMA((len(GROUPS),)),
            pltpu.SemaphoreType.DMA((len(GROUPS),)),
            pltpu.SemaphoreType.DMA((len(GROUPS), 7)),
            pltpu.SemaphoreType.DMA((len(GROUPS), 7)),
        ],
        compiler_params=pltpu.CompilerParams(
            collective_id=0, has_side_effects=True, vmem_limit_bytes=56 * 1024 * 1024
        ),
        cost_estimate=pl.CostEstimate(
            flops=15_000_000_000, bytes_accessed=8_000_000, transcendentals=6_300_000
        ),
        name="sparse_latent_attention",
    )(latent_cache, queries, chosen.T, key_up, value_up)


def solution(mesh):
    return jax.shard_map(
        on_device,
        mesh=mesh,
        in_specs=(
            P("ctx", None),
            P("ctx", "head"),
            P("ctx", None),
            P("head", None, None),
            P("head", None, None),
        ),
        out_specs=P("ctx", "head"),
        check_vma=False,
    )
```

time: 93.4 us -> 67.6 us (0.72)
  Pallas kernels: 89.9 us -> 65.5 us
  local copies, waits for them, and re-layouts: 3.33 us -> 1.88 us
    pallas_call x1, Pallas kernels: 89.9 us -> 65.5 us  [on_device(): pl.pallas_call(kernel, out_shape=jax.ShapeDtypeStruct((ROWS, HEADS * 128)...]
    unnamed x2 -> x1, local copies, waits for them, and re-layouts: 3.33 us -> 1.88 us
where the time goes in v2:
time: 67.6 us; the launch traced here: 67.4 us
  Pallas kernels  65.5 us (97%)
  local copies, waits for them, and re-layouts  1.88 us (3%)
    pallas_call x1, Pallas kernels, on_device(): pl.pallas_call(kernel, out_shape=jax.ShapeDtypeStruct((ROWS, HEADS * 128)...  65.5 us
    unnamed x1, local copies, waits for them, and re-layouts  1.88 us

profile of v2, /device:TPU:1, one launch (start us, length us, event | category | flops | bytes accessed | tf_op | source)
XLA Modules:
  0.0 67.4 jit_solution(248369819064559937)
XLA Ops:
  0.0 65.5 %sparse_latent_attention.1 = bf16[128,2048]{1,0:T(8,128)(2,1)} custom-call(bf16[64,36864]{1,0:T(8,128)(2,1)} %cache_hbm.1, bf16[128,3072]{1,0:T(8,128)(2,1)} %queries_hbm.1, s32[32,128]{1,0:T(8,128)} %bitcast.1, bf16[16,128,512]{2,1,0:T(8,128)(2,1)} %kup_hbm.1, bf16[16,512,128]{2,1,0:T(8,128)(2,1)} %vup_hbm.1), custom_call_target="tpu_custom_call" | custom-call | flops 15000000512 | bytes 8000000 | tf_op jit(solution)/shard_map/sparse_latent_attention/pallas_call | solution.py:389
  65.6 1.9 %copy.7 = bf16[128,2048]{1,0:T(8,128)(2,1)} copy(bf16[128,2048]{1,0:T(8,128)(2,1)} %sparse_latent_attention.1) | data formatting | bytes 1048576

commit v3 on v2

v3 whole, which is shorter than its diff:
```python
import functools

import jax
import jax.numpy as jnp
from jax import lax
from jax.experimental import pallas as pl
from jax.experimental.pallas import tpu as pltpu
from jax.sharding import PartitionSpec as P

BF = jnp.bfloat16
F32 = jnp.float32
CTX = 32
HEADS = 16
ROWS = 128
BD = 64
CAP = 3
POOL = 44
SLOTS = 48
SHARE = 4608
KEYS = 8 * SLOTS
CHUNKS = ((0, 1), (2, 3), (4,), (5, 6), (7,))
TILES = 7
AHEAD = 3
HP = 8
HIDE = -1e30
SCALE = (192**-0.5) * 1.4426950408889634


def nn(a, b):
    return lax.dot_general(a, b, (((1,), (0,)), ((), ())), preferred_element_type=F32)


def nt(a, b):
    return lax.dot_general(a, b, (((1,), (1,)), ((), ())), preferred_element_type=F32)


def iota(shape, dim):
    return lax.broadcasted_iota(jnp.int32, shape, dim)


def ones(cond):
    return jnp.where(cond, 1.0, 0.0).astype(BF)


def slot_of_row(r):
    return jnp.where(r < 5, 0, jnp.where(r < 10, 1, 2))


def kernel(
    cache_hbm, queries_hbm, chosen_hbm, kup_hbm, vup_hbm, out_hbm,
    shard, qraw, picks, kup, vup, req_send, req_recv, pack_send, pack_recv,
    pool, slot_oh, qext, acc, top, total, result,
    in_sem, req_sem, pack_ssem, pack_rsem, gat_ssem, gat_rsem, out_sem,
):
    me = lax.axis_index("ctx")
    hd = lax.axis_index("head")
    core = lax.rem(hd, 2)
    up = lax.rem(hd + 2, 8)
    down = lax.rem(hd + 6, 8)
    mate = hd + 1 - 2 * core
    far = lax.rem(hd + 4, 8)

    loads = []
    for n, (src, dst) in enumerate(
        (
            (chosen_hbm, picks),
            (cache_hbm.at[:, pl.ds(pl.multiple_of(hd * SHARE, 128), SHARE)], shard),
            (queries_hbm, qraw),
            (kup_hbm, kup),
            (vup_hbm, vup),
        )
    ):
        load = pltpu.make_async_copy(src, dst, in_sem.at[n])
        load.start()
        loads.append(load)

    barrier = pltpu.get_barrier_semaphore()

    def greet(k, carry):
        pl.semaphore_signal(barrier, inc=1, device_id={"ctx": lax.rem(me + k, CTX)})
        return carry

    lax.fori_loop(1, CTX, greet, 0)
    for peer in (up, down, far, mate):
        pl.semaphore_signal(barrier, inc=1, device_id={"head": peer})

    loads[0].wait()
    pick = picks[...]
    hi, lo = lax.shift_right_logical(pick, 6), pick & 63
    own_i = iota((CTX, ROWS), 0)
    blk_i = iota((128, ROWS), 0) & 63
    hi_oh = jnp.concatenate([ones(hi[j : j + 1] == own_i) for j in range(32)], axis=1)
    lo_oh = jnp.concatenate([ones(lo[j : j + 1] == blk_i) for j in range(32)], axis=1)
    flags = ones(nt(hi_oh, lo_oh) > 0.5)
    lane_r, lane_c = iota((128, 128), 0), iota((128, 128), 1)
    upto = ones((lane_r <= lane_c) & ((lane_r >> 6) == (lane_c >> 6)))
    rank = nn(flags, upto)
    hit = [(flags.astype(F32) > 0.5) & (rank == float(c + 1)) for c in range(CAP)]
    order = jnp.where(flags.astype(F32) > 0.5, rank, 0.0)
    for o in range(CTX):
        req_send[o] = order[o : o + 1]
    req_recv[me] = req_send[me]
    mine = pl.ds(pl.multiple_of(me * 16, 16), 16)

    pl.semaphore_wait(barrier, CTX - 1 + 4)

    def ask(k, carry):
        to = lax.rem(me + k, CTX)
        pltpu.make_async_remote_copy(
            src_ref=req_send.at[to],
            dst_ref=req_recv.at[me],
            send_sem=req_sem.at[0],
            recv_sem=req_sem.at[1],
            device_id={"ctx": to},
        ).start()
        return carry

    lax.fori_loop(1, CTX, ask, 0)

    n_lane = nt(jnp.ones((8, 128), BF), flags) * 0.5
    wide_o, wide_l = iota((CTX, CTX * 16), 0), iota((CTX, CTX * 16), 1) >> 4
    count = nn(n_lane.astype(BF), ones(wide_o == wide_l))[:1]
    base = nn(n_lane.astype(BF), ones(wide_o < wide_l))[:1]
    row_l = iota((1, CTX * 16), 1) & 15
    slot_s = iota((SLOTS, CTX * 16), 0).astype(F32)

    def place(c, rows):
        return ones(jnp.where(rows & (c < count), base + c, -1.0) == slot_s)

    c_row = slot_of_row(row_l)
    part = row_l - 5 * c_row
    spread = jnp.concatenate(
        [place(c_row.astype(F32), (row_l < 15) & (part == i)) for i in range(5)], axis=0
    )
    rest = [place(float(c), row_l == 15) for c in range(CAP)]

    n_row = n_lane[:1]
    base_row = nn(n_lane.astype(BF), ones(iota((CTX, CTX), 0) < iota((CTX, CTX), 1)))[:1]
    lane_v = iota((8, 128), 1)
    block_v = jnp.where(lane_v < 64, lane_v, 0).astype(F32).astype(BF)
    slot_c = iota((SLOTS, CTX), 0).astype(F32)
    owner_v = iota((1, CTX), 1).astype(F32) * 64.0
    ids = jnp.zeros((SLOTS, CTX), F32)
    for c in range(CAP):
        ident = owner_v + nt(block_v, ones(hit[c]))[:1]
        at = jnp.where(float(c) < n_row, base_row + float(c), -1.0) == slot_c
        ids = ids + jnp.where(at, ident, 0.0)
    ids = jnp.broadcast_to(jnp.sum(ids, axis=1, keepdims=True), (SLOTS, ROWS))
    pick_f = pick.astype(F32)
    found = jnp.zeros((SLOTS, ROWS), F32)
    for j in range(32):
        found = jnp.where(pick_f[j : j + 1] == ids, 1.0, found)
    hidden = jnp.where((found < 0.5) | (iota((SLOTS, ROWS), 0) >= POOL), HIDE, 0.0)
    hide = jnp.concatenate([hidden, jnp.zeros((ROWS - SLOTS, ROWS), F32)], axis=0).T.astype(BF)

    loads[2].wait()
    loads[3].wait()
    lane_q = iota((ROWS, 128), 1)
    for pair in range(HEADS // 2):
        a, b, c = [
            qraw[:, (3 * pair + i) * 128 : (3 * pair + i + 1) * 128].astype(F32) for i in range(3)
        ]
        b_r, c_r = pltpu.roll(b, 64, 1), pltpu.roll(c, 64, 1)
        halves = (
            (a, jnp.where(lane_q < 64, b, b_r)),
            (jnp.where(lane_q < 64, b_r, c_r), jnp.where(lane_q < 64, c_r, c)),
        )
        for k, (nope, rope) in enumerate(halves):
            h = 2 * pair + k
            qext[h, :, :512] = nn(nope.astype(BF), kup[h]).astype(BF)
            qext[h, :, 512:640] = rope.astype(BF)
            qext[h, :, 640:] = hide
    slot_oh[...] = ones(iota((8, SLOTS, 128), 1) == iota((8, SLOTS, 128), 2)).reshape(KEYS, 128)

    loads[1].wait()
    pltpu.make_async_remote_copy(
        src_ref=req_send.at[pl.ds(0, CTX - 1)],
        dst_ref=req_recv.at[pl.ds(0, CTX - 1)],
        send_sem=req_sem.at[0],
        recv_sem=req_sem.at[1],
        device_id={"ctx": me},
    ).wait_recv()
    rep = ones((iota((CTX * 16, CTX), 0) >> 4) == iota((CTX * 16, CTX), 1))
    got = nn(rep, req_recv[:, 0, :].astype(BF))
    row = iota((CTX * 16, 128), 0) & 15
    lane = iota((CTX * 16, 128), 1)
    c_of = slot_of_row(row)
    asked = (got == (c_of + 1).astype(F32)) & (row < 15)
    sel = [ones(asked & (row - 5 * c_of == 2 * k + (lane >> 6))) for k in range(3)]
    spare = [ones((row == 15) & (lane >= 64) & (got == float(c + 1))) for c in range(CAP)]

    def tile(u):
        return shard[:, u * 128 : u * 128 + 128]

    def give(t):
        def one(k, carry):
            to = lax.rem(me + k, CTX)
            pltpu.make_async_remote_copy(
                src_ref=pack_send.at[t, pl.ds(pl.multiple_of(to * 16, 16), 16), :],
                dst_ref=pack_recv.at[t, mine, :],
                send_sem=pack_ssem.at[t],
                recv_sem=pack_rsem.at[t],
                device_id={"ctx": to},
            ).start()
            return carry

        lax.fori_loop(1, CTX, one, 0)

    for t in range(TILES):
        if t < 6:
            last = sel[2] + spare[t % 3]
            src = [tile(5 * t + i) for i in range(5)] + [tile(30 + t // 3)]
        else:
            last = sel[2]
            src = [tile(min(32 + i, 35)) for i in range(6)]
        packed = nn(jnp.concatenate(sel[:2] + [last], axis=1), jnp.concatenate(src, axis=0))
        pack_send[t] = packed.astype(BF)
        pack_recv[t, mine, :] = pack_send[t, mine, :]
        if t < AHEAD:
            give(t)

    def gather_copy(p, kind, piece, to):
        part = pool.at[p, piece]
        return pltpu.make_async_remote_copy(
            src_ref=part,
            dst_ref=part,
            send_sem=gat_ssem.at[p, kind],
            recv_sem=gat_rsem.at[p, kind],
            device_id={"head": to},
        )

    started = []

    def send(p, kind, piece, to):
        copy = gather_copy(p, kind, piece, to)
        copy.start()
        started.append(copy)

    tiles = {}
    lane48 = iota((SLOTS, 128), 1)

    def share(p):
        u = 9 * (p // 2)
        if p % 2 == 0:
            cols = [tiles[u + k] for k in range(4)]
            cols.append(jnp.where(lane48 < 64, tiles[u + 4], 0.0))
        else:
            r = [pltpu.roll(tiles[u + k], 64, 1) for k in range(4, 9)]
            cols = [jnp.where(lane48 < 64, r[k], r[k + 1]) for k in range(4)]
            cols.append(jnp.where(lane48 < 64, 0.0, tiles[u + 8]))
        pool[p, hd] = jnp.concatenate(cols, axis=1).astype(BF)
        send(p, 0, hd, up)
        send(p, 1, hd, down)
        send(p, 2, hd, far)
        send(p, 3, hd, mate)

    def arrive(t):
        pltpu.make_async_remote_copy(
            src_ref=pack_send.at[t, pl.ds(0, (CTX - 1) * 16), :],
            dst_ref=pack_recv.at[t, pl.ds(0, (CTX - 1) * 16), :],
            send_sem=pack_ssem.at[t],
            recv_sem=pack_rsem.at[t],
            device_id={"ctx": me},
        ).wait_recv()
        if t + AHEAD < TILES:
            give(t + AHEAD)
        moved = nn(spread, pack_recv[t])
        for i in range(5):
            tiles[5 * t + i if t < 6 else 32 + i] = moved[SLOTS * i : SLOTS * i + SLOTS]
        if t == 5:
            for k in range(2):
                tiles[30 + k] = sum(nn(rest[c], pack_recv[3 * k + c]) for c in range(CAP))
        for p in ((0,), (1,), (2,), (3,), (4,), (5, 6), (7,))[t]:
            share(p)

    def relay(p):
        for kind, piece in ((0, down), (1, up), (2, far)):
            gather_copy(p, kind, piece, piece).wait_recv()
            send(p, 4 + kind, piece, mate)

    def ready(j):
        for p in CHUNKS[j]:
            for kind in (3, 4, 5, 6):
                gather_copy(p, kind, mate, mate).wait_recv()

    def store_head(h):
        lanes = pl.ds(h * 128, 128)
        return pltpu.make_async_copy(result.at[:, lanes], out_hbm.at[:, lanes], out_sem.at[h])

    rows_step = HP * ROWS

    def attend(j, n):
        hs = pl.ds(n * HP, HP)
        wide = len(CHUNKS[j]) * KEYS // 128
        held = [pool[p].reshape(KEYS, 640) for p in CHUNKS[j]]
        whole = jnp.concatenate(
            [jnp.concatenate([x, slot_oh[...]], axis=1) for x in held], axis=0
        )
        keys = jnp.concatenate([x[:, :512] for x in held], axis=0)
        q = qext[hs].reshape(rows_step, 768)
        s = nt(q, whole)
        m_new = jnp.broadcast_to(jnp.max(s, axis=1, keepdims=True), (rows_step, 128))
        if j > 0:
            m_old = top[hs].reshape(rows_step, 128)
            m_new = jnp.maximum(m_new, m_old)
        e = jnp.exp2((s - jnp.concatenate([m_new] * wide, axis=1)) * SCALE)
        part_sum = sum(e[:, 128 * k : 128 * k + 128] for k in range(wide))
        o = nn(e.astype(BF), keys)
        if j > 0:
            alpha = jnp.exp2((m_old - m_new) * SCALE)
            part_sum = part_sum + total[hs].reshape(rows_step, 128) * alpha
            o = o + acc[hs].reshape(rows_step, 512) * jnp.concatenate([alpha] * 4, axis=1)
        if j < len(CHUNKS) - 1:
            top[hs] = m_new.reshape(HP, ROWS, 128)
            total[hs] = part_sum.reshape(HP, ROWS, 128)
            acc[hs] = o.reshape(HP, ROWS, 512)
        else:
            mixed = (o * (1.0 / jnp.sum(part_sum, axis=1, keepdims=True))).astype(BF)
            for k in range(HP):
                h = n * HP + k
                result[:, h * 128 : h * 128 + 128] = nn(
                    mixed[k * ROWS : (k + 1) * ROWS], vup[h]
                ).astype(BF)
                store_head(h).start()

    arrive(0)
    arrive(1)
    relay(0)
    arrive(2)
    relay(1)
    arrive(3)
    ready(0)
    attend(0, 0)
    relay(2)
    arrive(4)
    attend(0, 1)
    relay(3)
    arrive(5)
    ready(1)
    attend(1, 0)
    relay(4)
    arrive(6)
    attend(1, 1)
    relay(5)
    relay(6)
    ready(2)
    attend(2, 0)
    attend(2, 1)
    relay(7)
    ready(3)
    attend(3, 0)
    attend(3, 1)
    ready(4)
    loads[4].wait()
    attend(4, 0)
    attend(4, 1)

    for copy in started:
        copy.wait_send()
    for h in range(HEADS):
        store_head(h).wait()
    pltpu.make_async_remote_copy(
        src_ref=req_send.at[pl.ds(0, CTX - 1)],
        dst_ref=req_recv.at[pl.ds(0, CTX - 1)],
        send_sem=req_sem.at[0],
        recv_sem=req_sem.at[1],
        device_id={"ctx": me},
    ).wait_send()
    for t in range(TILES):
        pltpu.make_async_remote_copy(
            src_ref=pack_send.at[t, pl.ds(0, (CTX - 1) * 16), :],
            dst_ref=pack_recv.at[t, pl.ds(0, (CTX - 1) * 16), :],
            send_sem=pack_ssem.at[t],
            recv_sem=pack_rsem.at[t],
            device_id={"ctx": me},
        ).wait_send()


def on_device(latent_cache, queries, chosen, key_up, value_up):
    any_spec = pl.BlockSpec(memory_space=pl.ANY)
    return pl.pallas_call(
        kernel,
        out_shape=jax.ShapeDtypeStruct((ROWS, HEADS * 128), BF),
        in_specs=[any_spec] * 5,
        out_specs=any_spec,
        scratch_shapes=[
            pltpu.VMEM((BD, SHARE), BF),
            pltpu.VMEM((ROWS, HEADS * 192), BF),
            pltpu.VMEM((32, ROWS), jnp.int32),
            pltpu.VMEM((HEADS, 128, 512), BF),
            pltpu.VMEM((HEADS, 512, 128), BF),
            pltpu.VMEM((CTX, 1, 128), F32),
            pltpu.VMEM((CTX, 1, 128), F32),
            pltpu.VMEM((TILES, CTX * 16, 128), BF),
            pltpu.VMEM((TILES, CTX * 16, 128), BF),
            pltpu.VMEM((8, 8, SLOTS, 640), BF),
            pltpu.VMEM((KEYS, 128), BF),
            pltpu.VMEM((HEADS, ROWS, 768), BF),
            pltpu.VMEM((HEADS, ROWS, 512), F32),
            pltpu.VMEM((HEADS, ROWS, 128), F32),
            pltpu.VMEM((HEADS, ROWS, 128), F32),
            pltpu.VMEM((ROWS, HEADS * 128), BF),
            pltpu.SemaphoreType.DMA((5,)),
            pltpu.SemaphoreType.DMA((2,)),
            pltpu.SemaphoreType.DMA((TILES,)),
            pltpu.SemaphoreType.DMA((TILES,)),
            pltpu.SemaphoreType.DMA((8, 7)),
            pltpu.SemaphoreType.DMA((8, 7)),
            pltpu.SemaphoreType.DMA((HEADS,)),
        ],
        compiler_params=pltpu.CompilerParams(
            collective_id=0, has_side_effects=True, vmem_limit_bytes=56 * 1024 * 1024
        ),
        cost_estimate=pl.CostEstimate(
            flops=15_000_000_000, bytes_accessed=8_000_000, transcendentals=6_300_000
        ),
        name="sparse_latent_attention",
    )(latent_cache, queries, chosen.T, key_up, value_up)


def solution(mesh):
    return jax.shard_map(
        on_device,
        mesh=mesh,
        in_specs=(
            P("ctx", None),
            P("ctx", "head"),
            P("ctx", None),
            P("head", None, None),
            P("head", None, None),
        ),
        out_specs=P("ctx", "head"),
        check_vma=False,
    )
```

time: 67.6 us -> 64.5 us (0.954)
  Pallas kernels: 65.5 us -> 62.2 us
    pallas_call x1, Pallas kernels: 65.5 us -> 62.2 us  [on_device(): pl.pallas_call(kernel, out_shape=jax.ShapeDtypeStruct((ROWS, HEADS * 128)...]
where the time goes in v3:
time: 64.5 us; the launch traced here: 64.1 us
  Pallas kernels  62.2 us (96%)
  local copies, waits for them, and re-layouts  1.88 us (3%)
    pallas_call x1, Pallas kernels, on_device(): pl.pallas_call(kernel, out_shape=jax.ShapeDtypeStruct((ROWS, HEADS * 128)...  62.2 us
    unnamed x1, local copies, waits for them, and re-layouts  1.88 us

profile of v3, /device:TPU:1, one launch (start us, length us, event | category | flops | bytes accessed | tf_op | source)
XLA Modules:
  0.0 64.1 jit_solution(7385214220840655729)
XLA Ops:
  0.0 62.2 %sparse_latent_attention.1 = bf16[128,2048]{1,0:T(8,128)(2,1)} custom-call(bf16[64,36864]{1,0:T(8,128)(2,1)} %cache_hbm.1, bf16[128,3072]{1,0:T(8,128)(2,1)} %queries_hbm.1, s32[32,128]{1,0:T(8,128)} %bitcast.1, bf16[16,128,512]{2,1,0:T(8,128)(2,1)} %kup_hbm.1, bf16[16,512,128]{2,1,0:T(8,128)(2,1)} %vup_hbm.1), custom_call_target="tpu_custom_call" | custom-call | flops 15000000512 | bytes 8000000 | tf_op jit(solution)/shard_map/sparse_latent_attention/pallas_call | solution.py:381
  62.2 1.9 %copy.7 = bf16[128,2048]{1,0:T(8,128)(2,1)} copy(bf16[128,2048]{1,0:T(8,128)(2,1)} %sparse_latent_attention.1) | data formatting | bytes 1048576

commit v4 on v3

--- a/solution.py
+++ b/solution.py
@@ -342,9 +342,9 @@
     arrive(6)
     attend(1, 1)
     relay(5)
-    relay(6)
     ready(2)
     attend(2, 0)
+    relay(6)
     attend(2, 1)
     relay(7)
     ready(3)

time: 64.5 us -> 64.4 us (level)
  no operation moved by 1% of the time
where the time goes in v4:
time: 64.4 us; the launch traced here: 64.2 us
  Pallas kernels  62.3 us (97%)
  local copies, waits for them, and re-layouts  1.88 us (3%)
    pallas_call x1, Pallas kernels, on_device(): pl.pallas_call(kernel, out_shape=jax.ShapeDtypeStruct((ROWS, HEADS * 128)...  62.3 us
    unnamed x1, local copies, waits for them, and re-layouts  1.88 us

profile of v4, /device:TPU:1, one launch (start us, length us, event | category | flops | bytes accessed | tf_op | source)
XLA Modules:
  0.0 64.2 jit_solution(6307154980285050091)
XLA Ops:
  0.0 62.3 %sparse_latent_attention.1 = bf16[128,2048]{1,0:T(8,128)(2,1)} custom-call(bf16[64,36864]{1,0:T(8,128)(2,1)} %cache_hbm.1, bf16[128,3072]{1,0:T(8,128)(2,1)} %queries_hbm.1, s32[32,128]{1,0:T(8,128)} %bitcast.1, bf16[16,128,512]{2,1,0:T(8,128)(2,1)} %kup_hbm.1, bf16[16,512,128]{2,1,0:T(8,128)(2,1)} %vup_hbm.1), custom_call_target="tpu_custom_call" | custom-call | flops 15000000512 | bytes 8000000 | tf_op jit(solution)/shard_map/sparse_latent_attention/pallas_call | solution.py:381
  62.3 1.9 %copy.7 = bf16[128,2048]{1,0:T(8,128)(2,1)} copy(bf16[128,2048]{1,0:T(8,128)(2,1)} %sparse_latent_attention.1) | data formatting | bytes 1048576
